TPU v7x, 256 devices: a whole 4x4x8 slice. The times are simulated.
256 devices in a mesh: pole: 4 (over z_lo), prow: 8 (over x, core), pcol: 8 (over y, z_hi).
Axes of the slice: x: 4, y: 4, z: 8 (z_hi: 2, z_lo: 4; z = z_hi * 4 + z_lo), core: 2. Of those that a mesh axis runs over, the one named last changes fastest.
Arguments:
- lower: float32 [4, 4096, 4096], P('pole', 'prow', 'pcol'), may hold values from -0.1875 to 0.1875
- upper: float32 [4, 4096, 4096], P('pole', 'prow', 'pcol'), may hold values from -0.1875 to 0.1875
- dinv: float32 [4, 4096, 4096], P('pole', 'prow', 'pcol'), may hold values from -6 to 6
- pole_weight: float32 [4], P('pole'), may hold values from 0.25 to 1
- block_pattern: int32 [16, 16], replicated, may hold values 0 or 1
Outputs:
- density: float32 [4096, 4096], P('prow', 'pcol')
All inputs are finite; a program needn't handle non-finite values.
Results may differ from a plain program's by a relative error of at most 0.0001.
Values sent between devices are 32-bit elements; how exact they have to be, the bound alone decides.
A program may use at most 64 MiB of HBM per device.

v0:
```python
import jax
import jax.numpy as jnp
from jax import lax
from jax.sharding import PartitionSpec as P

B = 256


def tier_of(supers):
    halves = supers // 2
    upper_tier = jnp.where(halves < 4, 1, 2)
    return jnp.where(supers % 2 == 0, 0, upper_tier)


def node_of(supers):
    halves = supers // 2
    upper_node = jnp.where(halves < 4, halves // 2, 0)
    return jnp.where(supers % 2 == 0, halves // 2, upper_node)


def above(elders, youngers):
    tier_old = tier_of(elders)[:, None]
    tier_new = tier_of(youngers)[None, :]
    node_old = node_of(elders)[:, None]
    node_new = node_of(youngers)[None, :]
    shift_by = jnp.maximum(tier_old - tier_new, 0)
    return (tier_old > tier_new) & (node_old == jnp.right_shift(node_new, shift_by))


def same_node(firsts, seconds):
    tier_same = tier_of(firsts)[:, None] == tier_of(seconds)[None, :]
    node_same = node_of(firsts)[:, None] == node_of(seconds)[None, :]
    return tier_same & node_same


def highest(left, right):
    return jnp.dot(left, right, precision=lax.Precision.HIGHEST, preferred_element_type=jnp.float32)


def blockmul(values, mask):
    mask_rows, mask_cols = mask.shape
    shaped = values.reshape(
        mask_rows, values.shape[0] // mask_rows, mask_cols, values.shape[1] // mask_cols
    )
    return (shaped * mask[:, None, :, None].astype(values.dtype)).reshape(values.shape)


def quarter(values, row_slot, col_slot):
    height, breadth = values.shape
    shaped = values.reshape(height // (2 * B), 2, B, breadth // (2 * B), 2, B)
    return shaped[:, row_slot, :, :, col_slot, :].reshape(height // 2, breadth // 2)


def rows_in_slot(values, slot_now):
    height, breadth = values.shape
    return values.reshape(height // (2 * B), 2, B, breadth)[:, slot_now].reshape(
        height // 2, breadth
    )


def columns_in_slot(values, slot_now):
    height, breadth = values.shape
    return values.reshape(height, breadth // (2 * B), 2, B)[:, :, slot_now].reshape(
        height, breadth // 2
    )


def assemble(part_even, part_mixed, part_cross, part_odd):
    half_rows, half_cols = part_even.shape
    shape_four = (half_rows // B, B, half_cols // B, B)
    top_half = jnp.stack([part_even.reshape(shape_four), part_mixed.reshape(shape_four)], axis=3)
    bottom_half = jnp.stack([part_cross.reshape(shape_four), part_odd.reshape(shape_four)], axis=3)
    return jnp.stack([top_half, bottom_half], axis=1).reshape(2 * half_rows, 2 * half_cols)


def local(lower, upper, dinv, pole_weight, block_pattern):
    height, breadth = (lower.shape[1], lower.shape[2])
    row_blocks = height // B
    col_blocks = breadth // B
    row_sup = lax.axis_index("prow") * row_blocks + jnp.arange(row_blocks)
    col_sup = lax.axis_index("pcol") * col_blocks + jnp.arange(col_blocks)
    pattern_here = lax.dynamic_slice(
        block_pattern, (row_sup[0], col_sup[0]), (row_blocks, col_blocks)
    )
    pattern_flip = lax.dynamic_slice(
        block_pattern, (col_sup[0], row_sup[0]), (col_blocks, row_blocks)
    ).T
    keep_lower = above(row_sup, col_sup) & (pattern_here > 0)
    keep_upper = above(col_sup, row_sup).T & (pattern_flip > 0)
    row_odd = row_sup[1::2]
    col_odd = col_sup[1::2]
    root_mask = same_node(row_odd, col_odd) & (tier_of(row_odd)[:, None] == 2)
    empty = jnp.zeros((height // 2, breadth // 2), jnp.float32)
    weight = pole_weight[0]
    lmat = blockmul(lower[0], keep_lower)
    umat = blockmul(upper[0], keep_upper)
    lower_panel = lax.all_gather(rows_in_slot(lmat, 1), "prow", axis=0, tiled=True)
    upper_panel = lax.all_gather(columns_in_slot(umat, 1), "pcol", axis=1, tiled=True)
    greens_odd = blockmul(quarter(dinv[0], 1, 1), root_mask)
    panel = empty
    rowpart = empty
    diagpart = empty
    for tier_now in (1, 0):
        slot_now = 0 if tier_now == 0 else 1
        row_tier = row_sup[slot_now::2]
        col_tier = col_sup[slot_now::2]
        left_factor = columns_in_slot(lower_panel, slot_now)
        right_factor = rows_in_slot(upper_panel, slot_now)

        def along_columns(piece):
            return highest(right_factor, piece)

        folded_rows = highest(lax.all_gather(greens_odd, "pcol", axis=1, tiled=True), left_factor)
        col_flags = tier_of(col_tier) == tier_now
        row_flags = tier_of(row_tier) == tier_now
        panel = -blockmul(folded_rows, above(row_odd, col_tier) & col_flags[None, :])
        folded_columns = along_columns(lax.all_gather(greens_odd, "prow", axis=0, tiled=True))
        rowpart = -blockmul(folded_columns, above(col_odd, row_tier).T & row_flags[:, None])
        correction = along_columns(lax.all_gather(panel, "prow", axis=0, tiled=True))
        share = same_node(row_tier, col_tier) & row_flags[:, None]
        diagpart = blockmul(quarter(dinv[0], slot_now, slot_now) - correction, share)
        if tier_now > 0:
            greens_odd = greens_odd + panel + rowpart + diagpart
    density = weight * assemble(diagpart, rowpart, panel, greens_odd)
    return lax.psum(density, "pole")


def solution(mesh):
    in_specs = (
        P("pole", "prow", "pcol"),
        P("pole", "prow", "pcol"),
        P("pole", "prow", "pcol"),
        P("pole"),
        P(),
    )
    out_specs = P("prow", "pcol")
    return jax.shard_map(local, mesh=mesh, in_specs=in_specs, out_specs=out_specs, check_vma=False)
```

profile of v0, /device:TPU:1, one launch (start us, length us, event | category | flops | bytes accessed | tf_op | source)
XLA Modules:
  0.0 553.8 jit_solution(16048855129079267908)
XLA Ops:
  6.5 0.0 copy-start.3
  6.5 0.0 all-gather.25.cloned.1.call-start
  6.6 0.6 fusion.72
  8.6 0.6 fusion.71
  10.5 0.1 broadcast_subtract_fusion
  10.6 0.1 copy.16
  12.0 0.8 fusion.67
  12.8 0.1 copy.19
  12.9 0.8 and_convert_fusion
  13.7 0.1 broadcast_bitcast_fusion
  13.8 1.9 slice_multiply_fusion
  15.7 0.0 all-gather.25.cloned.1.call-update
  15.7 0.0 all-gather.11.cloned.1.call-start
  21.1 0.0 copy-done.3
  21.1 0.7 reshape_squeeze.33
  21.7 0.0 copy-start.4
  21.8 0.5 fusion.70
  22.2 0.7 fusion.66
  22.9 0.0 all-gather.11.cloned.1.call-update
  23.0 0.0 all-gather.23.cloned.1.call-start
  23.0 0.1 copy.14
  23.1 0.1 slice.61
  23.3 0.0 copy-done.4
  23.3 0.7 reshape_squeeze.35
  24.0 1.5 slice_multiply_fusion.1
  25.5 0.0 all-gather.23.cloned.1.call-update
  25.5 0.0 all-gather.15.cloned.1.call-start
  25.6 29.1 %all-gather.25.cloned.1.call-done = f32[1,1,2048,512]{3,2,1,0:T(8,128)} async-done(((f32[1,1,256,512]{3,2,1,0:T(8,128)}), f32[1,1,2048,512]{3,2,1,0:T(8,128)}) %all-gather.25.cloned.1.call-update) | async-done | bytes 4194320 | tf_op jit(solution)/shard_map/all_gather | solution.py:97
  54.7 5.9 %reshape.388 = f32[2048,1,2,256]{3,2,0,1:T(2,128)} reshape(f32[1,1,2048,512]{3,2,1,0:T(8,128)} %all-gather.25.cloned.1.call-done) | data formatting | bytes 8388608 | tf_op jit(solution)/shard_map/reshape | solution.py:63
  60.6 7.6 %fusion.69 = (f32[2048,1,1,256]{3,2,0,1:T(1,128)}, f32[2048,1,1,256]{3,2,0,1:T(1,128)S(1)}) fusion(f32[2048,1,2,256]{3,2,0,1:T(2,128)} %reshape.388), kind=kLoop, calls=%fused_computation.77 | loop fusion | bytes 8388608 | tf_op jit(solution)/shard_map/slice | solution.py:63
  68.2 64.3 %all-gather.11.cloned.1.call-done = f32[256,2048]{1,0:T(8,128)} async-done(((f32[256,256]{1,0:T(8,128)}), f32[256,2048]{1,0:T(8,128)}) %all-gather.11.cloned.1.call-update) | async-done | bytes 2097168 | tf_op jit(solution)/shard_map/all_gather | solution.py:113
  132.5 4.2 fusion.39
  136.7 0.0 all-gather.15.cloned.1.call-update
  136.7 0.0 all-gather.13.cloned.1.call-start
  136.8 0.5 all-gather.13.cloned.1.call-update
  137.3 0.2 all-gather.17.cloned.1.call-start
  137.6 144.1 %all-gather.23.cloned.1.call-done = f32[512,1,1,2048]{3,2,0,1:T(1,128)} async-done(((f32[512,1,1,256]{3,2,0,1:T(1,128)}), f32[512,1,1,2048]{3,2,0,1:T(1,128)}) %all-gather.23.cloned.1.call-update) | async-done | bytes 4194320 | tf_op jit(solution)/shard_map/all_gather | solution.py:98
  281.7 6.5 %fusion.68 = (f32[1,1,256,2048]{3,0,2,1:T(1,128)S(1)}, f32[1,1,256,2048]{3,0,2,1:T(1,128)}) fusion(f32[1,2,256,2048]{3,0,2,1:T(1,128)} %bitcast.118), kind=kLoop, calls=%fused_computation.76 | loop fusion | bytes 8388608 | tf_op jit(solution)/shard_map/slice | solution.py:56
  288.1 19.3 %all-gather.15.cloned.1.call-done = f32[2048,256]{1,0:T(8,128)} async-done(((f32[256,256]{1,0:T(8,128)}), f32[2048,256]{1,0:T(8,128)}) %all-gather.15.cloned.1.call-update) | async-done | bytes 2097168 | tf_op jit(solution)/shard_map/all_gather | solution.py:119
  307.4 4.6 fusion.57
  312.0 25.2 %all-gather.13.cloned.1.call-done = f32[2048,256]{1,0:T(8,128)} async-done(((f32[256,256]{1,0:T(8,128)}), f32[2048,256]{1,0:T(8,128)}) %all-gather.13.cloned.1.call-update) | async-done | bytes 2097168 | tf_op jit(solution)/shard_map/all_gather | solution.py:117
  337.2 0.0 copy-done
  337.2 0.0 copy-done.2
  337.2 5.2 fusion.51
  342.4 0.0 all-gather.17.cloned.1.call-update
  342.5 0.0 all-gather.21.cloned.1.call-start
  342.5 0.7 all-gather.21.cloned.1.call-update
  343.2 0.0 all-gather.19.cloned.1.call-start
  345.8 72.5 %all-gather.17.cloned.1.call-done = f32[256,2048]{1,0:T(8,128)} async-done(((f32[256,256]{1,0:T(8,128)}), f32[256,2048]{1,0:T(8,128)}) %all-gather.17.cloned.1.call-update) | async-done | bytes 2097168 | tf_op jit(solution)/shard_map/all_gather | solution.py:113
  418.3 4.9 fusion.63
  423.1 0.0 all-gather.19.cloned.1.call-update
  423.2 0.3 all-reduce.2.cloned.1.call-start
  426.9 0.0 copy-done.1
  426.9 1.0 maximum_bitcast_fusion.1
  427.9 17.4 %all-gather.21.cloned.1.call-done = f32[2048,256]{1,0:T(8,128)} async-done(((f32[256,256]{1,0:T(8,128)}), f32[2048,256]{1,0:T(8,128)}) %all-gather.21.cloned.1.call-update) | async-done | bytes 2097168 | tf_op jit(solution)/shard_map/all_gather | solution.py:117
  445.3 3.9 fusion.33
  449.2 26.0 %all-gather.19.cloned.1.call-done = f32[2048,256]{1,0:T(8,128)} async-done(((f32[256,256]{1,0:T(8,128)}), f32[2048,256]{1,0:T(8,128)}) %all-gather.19.cloned.1.call-update) | async-done | bytes 2097168 | tf_op jit(solution)/shard_map/all_gather | solution.py:119
  475.2 3.9 fusion.24
  479.2 0.1 maximum_multiply_fusion
  479.3 0.8 copy.20
  480.1 1.0 copy.30
  481.2 0.0 all-reduce.2.cloned.1.call-update
  481.2 63.8 %all-reduce.2.cloned.1.call-done = f32[512,512]{1,0:T(8,128)} async-done(((f32[512,512]{1,0:T(8,128)}), f32[512,512]{1,0:T(8,128)}) %all-reduce.2.cloned.1.call-update) | async-done | bytes 1048592 | tf_op jit(solution)/shard_map/psum | solution.py:125
  545.0 2.3 copy.97
  (11 shorter events, 0.1 us)
Async XLA Ops:
  6.5 14.5 %copy-start.3 = (f32[1,512,512]{2,1,0:T(8,128)S(1)}, f32[1,512,512]{2,1,0:T(8,128)}, u32[]{:S(2)}) copy-start(f32[1,512,512]{2,1,0:T(8,128)} %param.7) | copy-start | bytes 3145732
  6.5 48.1 %all-gather.25.cloned.1.call-start = ((), (), s32[]{:S(2)}) async-start(), calls=%async_computation.8 | async-start | bytes 4718592 | tf_op jit(solution)/shard_map/all_gather | solution.py:97
  15.7 116.8 %all-gather.11.cloned.1.call-start = ((), (), s32[]{:S(2)}) async-start(), calls=%async_computation | async-start | bytes 2359296 | tf_op jit(solution)/shard_map/all_gather | solution.py:113
  21.7 1.5 copy-start.4
  23.0 258.7 %all-gather.23.cloned.1.call-start = ((), (), s32[]{:S(2)}) async-start(), calls=%async_computation.7 | async-start | bytes 4718592 | tf_op jit(solution)/shard_map/all_gather | solution.py:98
  25.5 281.9 %all-gather.15.cloned.1.call-start = ((), (), s32[]{:S(2)}) async-start(), calls=%async_computation.2 | async-start | bytes 2359296 | tf_op jit(solution)/shard_map/all_gather | solution.py:119
  136.7 200.5 %all-gather.13.cloned.1.call-start = ((), (), s32[]{:S(2)}) async-start(), calls=%async_computation.1 | async-start | bytes 2359296 | tf_op jit(solution)/shard_map/all_gather | solution.py:117
  137.3 280.9 %all-gather.17.cloned.1.call-start = ((), (), s32[]{:S(2)}) async-start(), calls=%async_computation.3 | async-start | bytes 2359296 | tf_op jit(solution)/shard_map/all_gather | solution.py:113
  307.4 29.8 %copy-start = (f32[256,256]{1,0:T(8,128)S(1)}, f32[256,256]{1,0:T(8,128)}, u32[]{:S(2)}) copy-start(f32[256,256]{1,0:T(8,128)} %fusion.66) | copy-start | bytes 786436
  307.4 29.8 %copy-start.2 = (f32[256,256]{1,0:T(8,128)S(1)}, f32[256,256]{1,0:T(8,128)}, u32[]{:S(2)}) copy-start(f32[256,256]{1,0:T(8,128)} %fusion.39) | copy-start | bytes 786436
  342.5 102.9 %all-gather.21.cloned.1.call-start = ((), (), s32[]{:S(2)}) async-start(), calls=%async_computation.5 | async-start | bytes 2359296 | tf_op jit(solution)/shard_map/all_gather | solution.py:117
  343.2 132.0 %all-gather.19.cloned.1.call-start = ((), (), s32[]{:S(2)}) async-start(), calls=%async_computation.4 | async-start | bytes 2359296 | tf_op jit(solution)/shard_map/all_gather | solution.py:119
  418.3 8.6 %copy-start.1 = (f32[256,256]{1,0:T(8,128)S(1)}, f32[256,256]{1,0:T(8,128)}, u32[]{:S(2)}) copy-start(f32[256,256]{1,0:T(8,128)} %fusion.51) | copy-start | bytes 786436
  423.2 121.9 %all-reduce.2.cloned.1.call-start = ((), (), s32[]{:S(2)}) async-start(), calls=%async_computation.6 | async-start | bytes 2097152 | tf_op jit(solution)/shard_map/psum | solution.py:125
Sparse Core Ops, SparseCore 0:
  15.8 38.8 all-gather.24
  57.2 75.3 all-gather.10
  135.0 146.6 all-gather.22
  283.4 24.0 all-gather.14
  309.1 28.0 all-gather.12
  342.6 75.6 all-gather.16
  420.1 25.1 all-gather.20
  447.2 28.0 all-gather.18
  481.3 63.6 all-reduce.1
where the time goes:
time: 555 us; the launch traced here: 554 us
  waiting for transfers between devices  463 us (83%)
  between operations  28.7 us (5%)
  local copies, waits for them, and re-layouts  27.7 us (5%)
  matrix products  26.7 us (5%)
  other arithmetic  6.91 us (1%)
    all_gather x1, waiting for transfers between devices, local(): lax.all_gather(columns_in_slot(umat, 1), 'pcol', axis=1, tiled=True)  144 us
    all_gather x2, waiting for transfers between devices, local(): lax.all_gather(greens_odd, 'pcol', axis=1, tiled=True)  137 us
    psum x1, waiting for transfers between devices, local(): return lax.psum(density, 'pole')  63.8 us
    all_gather x2, waiting for transfers between devices, local(): lax.all_gather(panel, 'prow', axis=0, tiled=True)  45.3 us
    all_gather x2, waiting for transfers between devices, local(): lax.all_gather(greens_odd, 'prow', axis=0, tiled=True)  42.6 us
    all_gather x1, waiting for transfers between devices, local(): lax.all_gather(rows_in_slot(lmat, 1), 'prow', axis=0, tiled=True)  29.1 us
    dot_general x6, matrix products, highest(): jnp.dot(left, right, precision=lax.Precision.HIGHEST, preferred_element_t...  26.7 us
  transfers between devices with their start and end apart: 9, of which 9 were waited for; matrix products, arithmetic and copies ran while one was open for 8% of the time, Pallas kernels for 0%

commit v1 on v0

v1 whole, which is shorter than its diff:
```python
import jax
import jax.numpy as jnp
from jax import lax
from jax.experimental import pallas as pl
from jax.experimental.pallas import tpu as pltpu
from jax.sharding import PartitionSpec as P

B = 256
H = B // 2
MESH = pl.DeviceIdType.MESH
N_SEND = 128


def split(values):
    high = values.astype(jnp.bfloat16)
    low = (values - high.astype(jnp.float32)).astype(jnp.bfloat16)
    return high, low


def block_dot(left, right):
    lh, ll = split(left)
    rh, rl = split(right)
    big = jnp.concatenate([lh, lh, ll], axis=1)
    tall = jnp.concatenate([rh, rl, rh], axis=0)
    return jnp.dot(big, tall, preferred_element_type=jnp.float32)


def kernel(
    low_ref, up_ref, din_ref, weight_ref, pat_ref, out_ref,
    row_o, row_u, col_la, col_lt, col_l1, col_gt, col_ga, col_pt, col_pa,
    part, inbox,
    send_sem, ro_sem, ru_sem, la_sem, lt_sem, l1_sem, gt_sem, ga_sem, pt_sem, pa_sem, red_sem,
):
    p = lax.axis_index("pole")
    i = lax.axis_index("prow")
    j = lax.axis_index("pcol")
    x, c = i // 2, i % 2
    y, h = j // 2, j % 2
    sib = (p, 2 * x + 1 - c, j)
    partner = (p, i, 2 * y + 1 - h)
    jp = 2 * y + 1 - h

    def xdev(xx):
        return (p, 2 * xx + c, j)

    def ydev(yy):
        return (p, i, 2 * yy + h)

    barrier = pltpu.get_barrier_semaphore()
    others = [sib, partner]
    for d in (1, 2, 3):
        others += [xdev((x + d) % 4), ydev((y + d) % 4), ((p + d) % 4, i, j)]
    for dev in others:
        pl.semaphore_signal(barrier, inc=1, device_id=dev, device_id_type=MESH)

    yes = p >= 0
    sends = []

    def send(cond, src, dst, rsem, dev):
        copy = pltpu.make_async_remote_copy(
            src_ref=src, dst_ref=dst, send_sem=send_sem.at[len(sends)], recv_sem=rsem,
            device_id=dev, device_id_type=MESH,
        )
        sends.append((cond, copy))
        pl.when(cond)(lambda: copy.start())

    def arrive(cond, dst, rsem):
        copy = pltpu.make_async_remote_copy(
            src_ref=dst, dst_ref=dst, send_sem=send_sem.at[0], recv_sem=rsem,
            device_id=sib, device_id_type=MESH,
        )
        pl.when(cond)(lambda: copy.wait_recv())

    def flag(a, b):
        return jnp.where(pat_ref[a, b] > 0, 1.0, 0.0).astype(jnp.float32)

    weight = weight_ref[0]
    low_oo = flag(2 * i + 1, 2 * j + 1)
    low_oe = flag(2 * i + 1, 2 * j)
    up_oo = flag(2 * j + 1, 2 * i + 1)
    up_eo = flag(2 * j + 1, 2 * i)

    top_row = x >= 2
    top_col = y >= 2
    odd_live = top_row | top_col | (x == y)
    col_live = top_row | (x == y // 2)
    row_live = top_col | (y == x // 2)
    diag_live = x == y
    even, odd = pl.ds(0, B), pl.ds(B, B)
    minus_y = (2 * (y // 2), 2 * (y // 2) + 1)

    @pl.when(top_row & ~top_col)
    def _():
        block = low_ref[0, odd, odd] * low_oo
        row_o[j] = block
        col_l1[i - 4] = block

    @pl.when(top_row & top_col)
    def _():
        block = din_ref[0, odd, odd]
        row_o[j] = block
        col_gt[i - 4] = block

    @pl.when(~top_row & top_col)
    def _():
        row_o[j] = up_ref[0, odd, odd] * up_oo

    @pl.when(~top_row & (x == y))
    def _():
        row_o[j] = din_ref[0, odd, odd]

    @pl.when(x == y // 2)
    def _():
        col_la[c] = low_ref[0, odd, even] * low_oe

    @pl.when(row_live)
    def _():
        row_u[j] = up_ref[0, even, odd] * up_eo

    pl.semaphore_wait(barrier, 11)

    def needs_o(src, dst):
        wide = jnp.where(x == 1, dst >= 1, yes)
        return (((src >= 2) & wide) | ((src < 2) & (dst // 2 == src))) & (top_row | (src >= 2) | (src == x))

    def needs_u(src, dst):
        live = (src >= 2) | (src == x // 2)
        return live & ((dst >= 2) | (dst == x // 2) | (dst == x))

    def row_send(buf, sem, needs, slot):
        for d in (1, 3, 2):
            yy = (y + d) % 4
            send(needs(y, yy), buf.at[slot], buf.at[slot], sem.at[slot], ydev(yy))

    def row_arrive(buf, sem, needs, src):
        cond = needs(src, y) & (src != y)
        for half in (0, 1):
            slot = 2 * src + half
            arrive(cond, buf.at[slot], sem.at[slot])

    def col_send(buf, sem, base, live, needs):
        slot = i - base
        slot = jnp.where(live, slot, 0)
        for d in (1, 3, 2):
            xx = (x + d) % 4
            send(live & needs(xx), buf.at[slot], buf.at[slot], sem.at[slot], xdev(xx))
        send(live & needs(x), buf.at[slot], buf.at[slot], sem.at[slot], sib)

    def col_arrive(buf, sem, base, xs, live, needs):
        for xx in xs:
            near = 2 * xx + c - base
            far = 2 * xx + 1 - c - base
            cond = live(xx) & needs(x) & (xx != x)
            arrive(cond, buf.at[near], sem.at[near])
            send(cond, buf.at[near], buf.at[near], sem.at[near], sib)
        for xx in xs:
            far = 2 * xx + 1 - c - base
            arrive(live(xx) & needs(x), buf.at[far], sem.at[far])

    halves = ((0, p), (1, 3 - p))

    def toward(q, half):
        pole = q if half == 0 else 3 - q
        return (pole, i, j)

    def rows_of(quad, half):
        return pl.ds((quad // 2) * B + half * H, H), pl.ds((quad % 2) * B, B)

    def red_a(quad, live):
        for half, q in halves:
            src = part.at[quad, pl.ds(half * H, H)]
            send(live & (q == 0), src, inbox.at[quad, half, 0], red_sem.at[quad, half, 0], toward(1, half))
            send(live & (q == 3), src, inbox.at[quad, half, 1], red_sem.at[quad, half, 1], toward(2, half))

    def red_b(quad, live):
        for half, q in halves:
            arrive(live & (q == 2), inbox.at[quad, half, 1], red_sem.at[quad, half, 1])
            rows = pl.ds(half * H, H)

            @pl.when(live & (q == 2))
            def _():
                part[quad, rows] = part[quad, rows] + inbox[quad, half, 1]

            src = part.at[quad, rows]
            send(live & (q == 2), src, inbox.at[quad, half, 1], red_sem.at[quad, half, 1], toward(1, half))

    def red_c(quad, live):
        for half, q in halves:
            arrive(live & (q == 1), inbox.at[quad, half, 0], red_sem.at[quad, half, 0])
            arrive(live & (q == 1), inbox.at[quad, half, 1], red_sem.at[quad, half, 1])
            rows = pl.ds(half * H, H)
            orow, ocol = rows_of(quad, half)

            @pl.when(live & (q == 1))
            def _():
                out_ref[orow, ocol] = part[quad, rows] + inbox[quad, half, 0] + inbox[quad, half, 1]

            place = out_ref.at[orow, ocol]
            send(live & (q == 1), place, place, red_sem.at[quad, half, 2], toward(2, half))
            send(live & (q == 1), place, place, red_sem.at[quad, half, 2], toward(0, half))

    def red_d(quad, live):
        for half, q in halves:
            place = out_ref.at[rows_of(quad, half)]
            arrive(live & (q == 2), place, red_sem.at[quad, half, 2])
            send(live & (q == 2), place, place, red_sem.at[quad, half, 2], toward(3, half))

    def red_e(quad, live):
        for half, q in halves:
            place = out_ref.at[rows_of(quad, half)]
            arrive(live & ((q == 0) | (q == 3)), place, red_sem.at[quad, half, 2])

    def sum_dots(pairs):
        total = None
        for left, right in pairs:
            term = block_dot(left, right)
            total = term if total is None else total + term
        return total

    send(odd_live, row_o.at[j], row_o.at[j], ro_sem.at[j], partner)
    row_send(row_o, ro_sem, needs_o, j)
    la_live = x == y // 2
    la_needs = lambda xx: (xx >= 2) | (xx == y // 2)
    col_send(col_la, la_sem, 2 * (y // 2), la_live, la_needs)
    l1_live = top_row & ~top_col
    l1_needs = lambda xx: (xx >= 2) & (y < 2)
    col_send(col_l1, l1_sem, 4, l1_live, l1_needs)
    gt_needs = lambda xx: (y >= 2) | (xx // 2 == y) | ((xx == 1) & (y == 1))
    gt_any = lambda xx: xx >= 2
    col_send(col_gt, gt_sem, 4, top_row & top_col, gt_needs)

    @pl.when(~odd_live)
    def _():
        out_ref[odd, odd] = jnp.zeros((B, B), jnp.float32)

    @pl.when(~col_live)
    def _():
        out_ref[odd, even] = jnp.zeros((B, B), jnp.float32)

    @pl.when(~row_live)
    def _():
        out_ref[even, odd] = jnp.zeros((B, B), jnp.float32)

    @pl.when(~diag_live)
    def _():
        out_ref[even, even] = jnp.zeros((B, B), jnp.float32)

    arrive(odd_live, row_o.at[jp], ro_sem.at[jp])
    row_send(row_o, ro_sem, needs_o, jp)
    send(row_live, row_u.at[j], row_u.at[j], ru_sem.at[j], partner)
    row_send(row_u, ru_sem, needs_u, j)

    la_any = lambda xx: yes
    for shift in (0,):
        xx = y // 2
        near, far = c, 1 - c
        cond = la_needs(x) & (x != xx)
        arrive(cond, col_la.at[near], la_sem.at[near])
        send(cond, col_la.at[near], col_la.at[near], la_sem.at[near], sib)
        arrive(la_needs(x), col_la.at[far], la_sem.at[far])
    col_arrive(col_l1, l1_sem, 4, (2, 3), lambda xx: yes, l1_needs)
    for src in (0, 1):
        row_arrive(row_o, ro_sem, needs_o, src)

    @pl.when(top_row)
    def _():
        through = sum_dots([(row_o[minus_y[k]], col_la[k]) for k in (0, 1)])
        col_lt[i - 4] = low_ref[0, odd, even] * low_oe - through

    lt_needs = lambda xx: xx >= 2
    col_send(col_lt, lt_sem, 4, top_row, lt_needs)
    for src in (2, 3):
        row_arrive(row_o, ro_sem, needs_o, src)

    @pl.when(top_row & ~top_col)
    def _():
        col_gt[i - 4] = -sum_dots([(row_o[4 + k], col_l1[k]) for k in range(4)])

    col_send(col_gt, gt_sem, 4, top_row & ~top_col, gt_needs)

    @pl.when(top_row)
    def _():
        part[3] = col_gt[i - 4] * weight

    red_a(3, top_row)
    col_arrive(col_lt, lt_sem, 4, (2, 3), gt_any, lt_needs)

    @pl.when(top_row)
    def _():
        col_pt[i - 4] = -sum_dots([(row_o[4 + k], col_lt[k]) for k in range(4)])
        part[2] = col_pt[i - 4] * weight

    pt_needs = lambda xx: (xx == y // 2) | (xx == y)
    col_send(col_pt, pt_sem, 4, top_row, pt_needs)
    red_a(2, top_row)

    arrive(row_live, row_u.at[jp], ru_sem.at[jp])
    row_send(row_u, ru_sem, needs_u, jp)

    col_arrive(col_gt, gt_sem, 4, (2, 3), gt_any, gt_needs)
    ga_live = (x < 2) & (top_col | (x == y))

    @pl.when(ga_live)
    def _():
        base = jnp.where(x == y, 1.0, 0.0).astype(jnp.float32)
        folded = sum_dots([(row_o[4 + k], col_gt[k]) for k in range(4)])
        col_ga[c] = din_ref[0, odd, odd] * base - folded
        part[3] = col_ga[c] * weight

    for d in (1, 3, 2):
        xx = (x + d) % 4
        send(ga_live & (xx // 2 == x), col_ga.at[c], col_ga.at[2 + c], ga_sem.at[c], xdev(xx))
    send(ga_live & (x == 0), col_ga.at[c], col_ga.at[2 + c], ga_sem.at[c], sib)
    red_a(3, ga_live)

    col_arrive(col_pt, pt_sem, 4, (2, 3), gt_any, pt_needs)
    pa_live = x == y // 2

    @pl.when(pa_live)
    def _():
        near = sum_dots([(row_o[2 * x + k], col_la[k]) for k in (0, 1)])
        far = sum_dots([(row_o[4 + k], col_pt[k]) for k in range(4)])
        col_pa[c] = -(near + far)
        part[2] = col_pa[c] * weight

    for d in (1, 3, 2):
        xx = (x + d) % 4
        send(pa_live & (xx == y), col_pa.at[c], col_pa.at[c], pa_sem.at[c], xdev(xx))
    send(pa_live & (x == y), col_pa.at[c], col_pa.at[c], pa_sem.at[c], sib)
    red_a(2, pa_live)

    for src in (0, 1, 2, 3):
        row_arrive(row_u, ru_sem, needs_u, src)

    red_b(3, odd_live)
    red_b(2, col_live)
    red_c(3, odd_live)
    return_live = row_live
    cond = return_live & (x != 0)
    arrive(cond, col_ga.at[2 + c], ga_sem.at[c])
    send(cond, col_ga.at[2 + c], col_ga.at[2 + c], ga_sem.at[c], sib)
    arrive(return_live, col_ga.at[3 - c], ga_sem.at[1 - c])

    @pl.when(return_live & (x == 0))
    def _():
        col_ga[2 + c] = col_ga[c]

    @pl.when(row_live)
    def _():
        near = sum_dots([(row_u[2 * (x // 2) + k], col_ga[2 + k]) for k in (0, 1)])
        far = sum_dots([(row_u[4 + k], col_gt[k]) for k in range(4)])
        part[1] = -(near + far) * weight

    red_a(1, row_live)
    red_c(2, col_live)
    red_d(3, odd_live)

    cond = (x == y) & (x != y // 2)
    arrive(cond, col_pa.at[c], pa_sem.at[c])
    send(cond, col_pa.at[c], col_pa.at[c], pa_sem.at[c], sib)
    arrive(x == y, col_pa.at[1 - c], pa_sem.at[1 - c])

    @pl.when(diag_live)
    def _():
        near = sum_dots([(row_u[2 * (x // 2) + k], col_pa[k]) for k in (0, 1)])
        far = sum_dots([(row_u[4 + k], col_pt[k]) for k in range(4)])
        part[0] = (din_ref[0, even, even] - (near + far)) * weight

    red_a(0, diag_live)
    red_d(2, col_live)
    red_b(1, row_live)
    red_b(0, diag_live)
    red_c(1, row_live)
    red_c(0, diag_live)
    red_d(1, row_live)
    red_d(0, diag_live)
    red_e(3, odd_live)
    red_e(2, col_live)
    red_e(1, row_live)
    red_e(0, diag_live)

    assert len(sends) <= N_SEND
    for cond, copy in sends:
        pl.when(cond)(lambda copy=copy: copy.wait_send())


def local(lower, upper, dinv, pole_weight, block_pattern):
    vmem = pl.BlockSpec(memory_space=pltpu.VMEM)
    smem = pl.BlockSpec(memory_space=pltpu.SMEM)

    def blocks(*lead):
        return pltpu.VMEM(lead + (B, B), jnp.float32)

    def sems(*lead):
        return pltpu.SemaphoreType.DMA(lead)

    return pl.pallas_call(
        kernel,
        out_shape=jax.ShapeDtypeStruct((2 * B, 2 * B), jnp.float32),
        in_specs=[vmem, vmem, vmem, smem, smem],
        out_specs=vmem,
        scratch_shapes=[
            blocks(8), blocks(8), blocks(2), blocks(4), blocks(4), blocks(4), blocks(4), blocks(4), blocks(2),
            blocks(4), pltpu.VMEM((4, 2, 2, H, B), jnp.float32),
            sems(N_SEND), sems(8), sems(8), sems(2), sems(4), sems(4), sems(4), sems(2), sems(4), sems(2),
            sems(4, 2, 3),
        ],
        compiler_params=pltpu.CompilerParams(
            collective_id=0, has_side_effects=True, vmem_limit_bytes=48 * 2**20
        ),
    )(lower, upper, dinv, pole_weight, block_pattern)


def solution(mesh):
    in_specs = (
        P("pole", "prow", "pcol"),
        P("pole", "prow", "pcol"),
        P("pole", "prow", "pcol"),
        P("pole"),
        P(),
    )
    out_specs = P("prow", "pcol")
    return jax.shard_map(local, mesh=mesh, in_specs=in_specs, out_specs=out_specs, check_vma=False)
```

time: 555 us -> 107 us (0.19)
  waiting for transfers between devices: 463 us -> 0 us
  Pallas kernels: 0 us -> 101 us
  between operations: 28.7 us -> 0.67 us
  matrix products: 26.7 us -> 0 us
  local copies, waits for them, and re-layouts: 27.7 us -> 5.34 us
  other arithmetic: 6.91 us -> 0 us
    all_gather x8 -> x0, waiting for transfers between devices: 398 us -> none  [the longest x1 144 us: local(): lax.all_gather(columns_in_slot(umat, 1), 'pcol', axis=1, tiled=True)]
    pallas_call x0 -> x1, Pallas kernels: none -> 101 us  [local(): pl.pallas_call(kernel, out_shape=jax.ShapeDtypeStruct((2 * B, 2 * B), jnp...]
    psum x1 -> x0, waiting for transfers between devices: 63.8 us -> none  [local(): return lax.psum(density, 'pole')]
    dot_general x6 -> x0, matrix products: 26.7 us -> none  [highest(): jnp.dot(left, right, precision=lax.Precision.HIGHEST, preferred_element_t...]
    slice x7 -> x0, local copies, waits for them, and re-layouts: 15.9 us -> none  [the longest x2 7.74 us: columns_in_slot(): values.reshape(height, breadth // (2 * B), 2, B)[:, :, slot_now]]
    reshape x1 -> x0, local copies, waits for them, and re-layouts: 5.9 us -> none  [columns_in_slot(): values.reshape(height, breadth // (2 * B), 2, B)[:, :, slot_now]]
  transfers between devices with their start and end apart: 9 -> 0, of which waited for: 9 -> 0; matrix products, arithmetic and copies ran while one was open for 8% -> 0% of each run, Pallas kernels for 0% -> 0%
where the time goes in v1:
time: 107 us
  Pallas kernels  101 us (94%)
  local copies, waits for them, and re-layouts  5.34 us (5%)
    pallas_call x1, Pallas kernels, local(): pl.pallas_call(kernel, out_shape=jax.ShapeDtypeStruct((2 * B, 2 * B), jnp...  101 us
    unnamed x9, local copies, waits for them, and re-layouts  5.34 us

profile of v1, /device:TPU:1, one launch (start us, length us, event | category | flops | bytes accessed | tf_op | source)
XLA Modules:
  0.0 106.6 jit_solution(4751063976587925178)
XLA Ops:
  0.7 0.0 copy-start
  0.7 1.2 %copy-done = f32[1,512,512]{2,1,0:T(8,128)S(1)} copy-done((f32[1,512,512]{2,1,0:T(8,128)S(1)}, f32[1,512,512]{2,1,0:T(8,128)}, u32[]{:S(2)}) %copy-start) | copy-done | bytes 1048600
  1.9 0.0 copy-start.1
  1.9 1.2 %copy-done.1 = f32[1,512,512]{2,1,0:T(8,128)S(1)} copy-done((f32[1,512,512]{2,1,0:T(8,128)S(1)}, f32[1,512,512]{2,1,0:T(8,128)}, u32[]{:S(2)}) %copy-start.1) | copy-done | bytes 1048600
  3.1 0.0 copy-start.2
  3.1 1.2 %copy-done.2 = f32[1,512,512]{2,1,0:T(8,128)S(1)} copy-done((f32[1,512,512]{2,1,0:T(8,128)S(1)}, f32[1,512,512]{2,1,0:T(8,128)}, u32[]{:S(2)}) %copy-start.2) | copy-done | bytes 1048600
  4.3 0.0 copy-start.3
  4.3 0.7 copy-done.3
  5.0 100.6 %shard_map.55 = f32[512,512]{1,0:T(8,128)S(1)} custom-call(f32[1,512,512]{2,1,0:T(8,128)S(1)} %copy-done, f32[1,512,512]{2,1,0:T(8,128)S(1)} %copy-done.1, f32[1,512,512]{2,1,0:T(8,128)S(1)} %copy-done.2, f32[1]{0:T(128)S(6)} %copy.7.weight_ref, s32[16,16]{1,0:T(8,128)S(1)} %copy-done.3), custom_call_target="tpu_custom_call" | custom-call | tf_op jit(solution)/shard_map/pallas_call | solution.py:397
  105.6 1.0 copy.8
Async XLA Ops:
  0.7 1.2 %copy-start = (f32[1,512,512]{2,1,0:T(8,128)S(1)}, f32[1,512,512]{2,1,0:T(8,128)}, u32[]{:S(2)}) copy-start(f32[1,512,512]{2,1,0:T(8,128)} %low_ref.1) | copy-start | bytes 3145732
  1.9 1.2 %copy-start.1 = (f32[1,512,512]{2,1,0:T(8,128)S(1)}, f32[1,512,512]{2,1,0:T(8,128)}, u32[]{:S(2)}) copy-start(f32[1,512,512]{2,1,0:T(8,128)} %up_ref.1) | copy-start | bytes 3145732
  3.1 1.2 %copy-start.2 = (f32[1,512,512]{2,1,0:T(8,128)S(1)}, f32[1,512,512]{2,1,0:T(8,128)}, u32[]{:S(2)}) copy-start(f32[1,512,512]{2,1,0:T(8,128)} %din_ref.1) | copy-start | bytes 3145732
  4.3 0.7 copy-start.3

commit v2 on v1

--- a/solution.py
+++ b/solution.py
@@ -8,7 +8,7 @@
 B = 256
 H = B // 2
 MESH = pl.DeviceIdType.MESH
-N_SEND = 128
+N_SEND = 160
 
 
 def split(values):
@@ -28,7 +28,7 @@
 def kernel(
     low_ref, up_ref, din_ref, weight_ref, pat_ref, out_ref,
     row_o, row_u, col_la, col_lt, col_l1, col_gt, col_ga, col_pt, col_pa,
-    part, inbox,
+    part, inbox, raw_l, raw_d, in_sem,
     send_sem, ro_sem, ru_sem, la_sem, lt_sem, l1_sem, gt_sem, ga_sem, pt_sem, pa_sem, red_sem,
 ):
     p = lax.axis_index("pole")
@@ -49,9 +49,17 @@
     barrier = pltpu.get_barrier_semaphore()
     others = [sib, partner]
     for d in (1, 2, 3):
-        others += [xdev((x + d) % 4), ydev((y + d) % 4), ((p + d) % 4, i, j)]
+        others += [xdev((x + d) % 4), ydev((y + d) % 4)]
     for dev in others:
         pl.semaphore_signal(barrier, inc=1, device_id=dev, device_id_type=MESH)
+
+    @pl.when(p > 0)
+    def _():
+        pl.semaphore_signal(barrier, inc=1, device_id=(p - 1, i, j), device_id_type=MESH)
+
+    @pl.when(p < 3)
+    def _():
+        pl.semaphore_signal(barrier, inc=1, device_id=(p + 1, i, j), device_id_type=MESH)
 
     yes = p >= 0
     sends = []
@@ -89,35 +97,49 @@
     even, odd = pl.ds(0, B), pl.ds(B, B)
     minus_y = (2 * (y // 2), 2 * (y // 2) + 1)
 
-    @pl.when(top_row & ~top_col)
-    def _():
-        block = low_ref[0, odd, odd] * low_oo
+    mid_row = ~top_row & top_col
+    mid_col = top_row & ~top_col
+    loads = (
+        (mid_col, low_ref.at[0, odd, odd], row_o.at[j], 0),
+        (mid_row, up_ref.at[0, odd, odd], row_o.at[j], 0),
+        ((top_row & top_col) | (~top_row & (x == y)), din_ref.at[0, odd, odd], row_o.at[j], 0),
+        (col_live, low_ref.at[0, odd, even], raw_l, 1),
+        (row_live, up_ref.at[0, even, odd], row_u.at[j], 2),
+        (diag_live, din_ref.at[0, even, even], raw_d, 3),
+    )
+    loads = [(cond, pltpu.make_async_copy(src, dst, in_sem.at[k])) for cond, src, dst, k in loads]
+    for cond, copy in loads:
+        pl.when(cond)(lambda copy=copy: copy.start())
+    for cond, copy in loads:
+        pl.when(cond)(lambda copy=copy: copy.wait())
+
+    @pl.when(mid_col)
+    def _():
+        block = row_o[j] * low_oo
         row_o[j] = block
         col_l1[i - 4] = block
 
     @pl.when(top_row & top_col)
     def _():
-        block = din_ref[0, odd, odd]
-        row_o[j] = block
-        col_gt[i - 4] = block
-
-    @pl.when(~top_row & top_col)
-    def _():
-        row_o[j] = up_ref[0, odd, odd] * up_oo
-
-    @pl.when(~top_row & (x == y))
-    def _():
-        row_o[j] = din_ref[0, odd, odd]
+        col_gt[i - 4] = row_o[j]
+
+    @pl.when(mid_row)
+    def _():
+        row_o[j] = row_o[j] * up_oo
+
+    @pl.when(col_live)
+    def _():
+        raw_l[...] = raw_l[...] * low_oe
 
     @pl.when(x == y // 2)
     def _():
-        col_la[c] = low_ref[0, odd, even] * low_oe
+        col_la[c] = raw_l[...]
 
     @pl.when(row_live)
     def _():
-        row_u[j] = up_ref[0, even, odd] * up_eo
-
-    pl.semaphore_wait(barrier, 11)
+        row_u[j] = row_u[j] * up_eo
+
+    pl.semaphore_wait(barrier, jnp.where((p == 0) | (p == 3), 9, 10))
 
     def needs_o(src, dst):
         wide = jnp.where(x == 1, dst >= 1, yes)
@@ -227,7 +249,12 @@
     col_send(col_l1, l1_sem, 4, l1_live, l1_needs)
     gt_needs = lambda xx: (y >= 2) | (xx // 2 == y) | ((xx == 1) & (y == 1))
     gt_any = lambda xx: xx >= 2
-    col_send(col_gt, gt_sem, 4, top_row & top_col, gt_needs)
+    tt = top_row & top_col
+    col_send(col_gt, gt_sem, 4, tt, gt_needs)
+
+    @pl.when(tt)
+    def _():
+        part[3] = row_o[j] * weight
 
     @pl.when(~odd_live)
     def _():
@@ -249,6 +276,7 @@
     row_send(row_o, ro_sem, needs_o, jp)
     send(row_live, row_u.at[j], row_u.at[j], ru_sem.at[j], partner)
     row_send(row_u, ru_sem, needs_u, j)
+    red_a(3, tt)
 
     la_any = lambda xx: yes
     for shift in (0,):
@@ -265,24 +293,27 @@
     @pl.when(top_row)
     def _():
         through = sum_dots([(row_o[minus_y[k]], col_la[k]) for k in (0, 1)])
-        col_lt[i - 4] = low_ref[0, odd, even] * low_oe - through
+        col_lt[i - 4] = raw_l[...] - through
 
     lt_needs = lambda xx: xx >= 2
     col_send(col_lt, lt_sem, 4, top_row, lt_needs)
     for src in (2, 3):
         row_arrive(row_o, ro_sem, needs_o, src)
 
+    arrive(row_live, row_u.at[jp], ru_sem.at[jp])
+    row_send(row_u, ru_sem, needs_u, jp)
+
     @pl.when(top_row & ~top_col)
     def _():
         col_gt[i - 4] = -sum_dots([(row_o[4 + k], col_l1[k]) for k in range(4)])
 
     col_send(col_gt, gt_sem, 4, top_row & ~top_col, gt_needs)
 
-    @pl.when(top_row)
+    @pl.when(mid_col)
     def _():
         part[3] = col_gt[i - 4] * weight
 
-    red_a(3, top_row)
+    red_a(3, mid_col)
     col_arrive(col_lt, lt_sem, 4, (2, 3), gt_any, lt_needs)
 
     @pl.when(top_row)
@@ -293,18 +324,15 @@
     pt_needs = lambda xx: (xx == y // 2) | (xx == y)
     col_send(col_pt, pt_sem, 4, top_row, pt_needs)
     red_a(2, top_row)
-
-    arrive(row_live, row_u.at[jp], ru_sem.at[jp])
-    row_send(row_u, ru_sem, needs_u, jp)
+    red_b(3, tt)
 
     col_arrive(col_gt, gt_sem, 4, (2, 3), gt_any, gt_needs)
     ga_live = (x < 2) & (top_col | (x == y))
 
     @pl.when(ga_live)
     def _():
-        base = jnp.where(x == y, 1.0, 0.0).astype(jnp.float32)
         folded = sum_dots([(row_o[4 + k], col_gt[k]) for k in range(4)])
-        col_ga[c] = din_ref[0, odd, odd] * base - folded
+        col_ga[c] = jnp.where(x == y, row_o[j], 0.0) - folded
         part[3] = col_ga[c] * weight
 
     for d in (1, 3, 2):
@@ -312,6 +340,9 @@
         send(ga_live & (xx // 2 == x), col_ga.at[c], col_ga.at[2 + c], ga_sem.at[c], xdev(xx))
     send(ga_live & (x == 0), col_ga.at[c], col_ga.at[2 + c], ga_sem.at[c], sib)
     red_a(3, ga_live)
+    red_c(3, tt)
+    red_b(3, mid_col)
+
 
     col_arrive(col_pt, pt_sem, 4, (2, 3), gt_any, pt_needs)
     pa_live = x == y // 2
@@ -328,13 +359,14 @@
         send(pa_live & (xx == y), col_pa.at[c], col_pa.at[c], pa_sem.at[c], xdev(xx))
     send(pa_live & (x == y), col_pa.at[c], col_pa.at[c], pa_sem.at[c], sib)
     red_a(2, pa_live)
+    red_b(2, top_row)
+    red_d(3, tt)
+
 
     for src in (0, 1, 2, 3):
         row_arrive(row_u, ru_sem, needs_u, src)
 
-    red_b(3, odd_live)
-    red_b(2, col_live)
-    red_c(3, odd_live)
+
     return_live = row_live
     cond = return_live & (x != 0)
     arrive(cond, col_ga.at[2 + c], ga_sem.at[c])
@@ -352,8 +384,10 @@
         part[1] = -(near + far) * weight
 
     red_a(1, row_live)
-    red_c(2, col_live)
-    red_d(3, odd_live)
+    red_b(3, ga_live)
+    red_c(3, mid_col)
+    red_c(2, top_row)
+    red_b(2, pa_live)
 
     cond = (x == y) & (x != y // 2)
     arrive(cond, col_pa.at[c], pa_sem.at[c])
@@ -364,11 +398,16 @@
     def _():
         near = sum_dots([(row_u[2 * (x // 2) + k], col_pa[k]) for k in (0, 1)])
         far = sum_dots([(row_u[4 + k], col_pt[k]) for k in range(4)])
-        part[0] = (din_ref[0, even, even] - (near + far)) * weight
+        part[0] = (raw_d[...] - (near + far)) * weight
 
     red_a(0, diag_live)
-    red_d(2, col_live)
+    red_c(3, ga_live)
+    red_c(2, pa_live)
+    red_d(3, mid_col)
+    red_d(2, top_row)
     red_b(1, row_live)
+    red_d(3, ga_live)
+    red_d(2, pa_live)
     red_b(0, diag_live)
     red_c(1, row_live)
     red_c(0, diag_live)
@@ -387,6 +426,7 @@
 def local(lower, upper, dinv, pole_weight, block_pattern):
     vmem = pl.BlockSpec(memory_space=pltpu.VMEM)
     smem = pl.BlockSpec(memory_space=pltpu.SMEM)
+    hbm = pl.BlockSpec(memory_space=pl.ANY)
 
     def blocks(*lead):
         return pltpu.VMEM(lead + (B, B), jnp.float32)
@@ -397,16 +437,16 @@
     return pl.pallas_call(
         kernel,
         out_shape=jax.ShapeDtypeStruct((2 * B, 2 * B), jnp.float32),
-        in_specs=[vmem, vmem, vmem, smem, smem],
+        in_specs=[hbm, hbm, hbm, smem, smem],
         out_specs=vmem,
         scratch_shapes=[
             blocks(8), blocks(8), blocks(2), blocks(4), blocks(4), blocks(4), blocks(4), blocks(4), blocks(2),
-            blocks(4), pltpu.VMEM((4, 2, 2, H, B), jnp.float32),
+            blocks(4), pltpu.VMEM((4, 2, 2, H, B), jnp.float32), blocks(), blocks(), sems(4),
             sems(N_SEND), sems(8), sems(8), sems(2), sems(4), sems(4), sems(4), sems(2), sems(4), sems(2),
             sems(4, 2, 3),
         ],
         compiler_params=pltpu.CompilerParams(
-            collective_id=0, has_side_effects=True, vmem_limit_bytes=48 * 2**20
+            collective_id=0, has_side_effects=True, vmem_limit_bytes=52 * 2**20
         ),
     )(lower, upper, dinv, pole_weight, block_pattern)
 

time: 107 us -> 99.9 us (0.934)
  local copies, waits for them, and re-layouts: 5.34 us -> 1.66 us
  Pallas kernels: 101 us -> 97.5 us
    unnamed x9 -> x3, local copies, waits for them, and re-layouts: 5.34 us -> 1.66 us
    pallas_call x1, Pallas kernels: 101 us -> 97.5 us  [local(): pl.pallas_call(kernel, out_shape=jax.ShapeDtypeStruct((2 * B, 2 * B), jnp...]
where the time goes in v2:
time: 99.9 us; the launch traced here: 99.8 us
  Pallas kernels  97.5 us (98%)
  local copies, waits for them, and re-layouts  1.66 us (2%)
    pallas_call x1, Pallas kernels, local(): pl.pallas_call(kernel, out_shape=jax.ShapeDtypeStruct((2 * B, 2 * B), jnp...  97.5 us

profile of v2, /device:TPU:1, one launch (start us, length us, event | category | flops | bytes accessed | tf_op | source)
XLA Modules:
  0.0 99.8 jit_solution(11964078230405814768)
XLA Ops:
  0.7 0.0 copy-start
  0.7 0.7 copy-done
  1.4 97.5 %shard_map.55 = f32[512,512]{1,0:T(8,128)S(1)} custom-call(f32[1,512,512]{2,1,0:T(8,128)} %low_ref.1, f32[1,512,512]{2,1,0:T(8,128)} %up_ref.1, f32[1,512,512]{2,1,0:T(8,128)} %din_ref.1, f32[1]{0:T(128)S(6)} %copy.7.weight_ref, s32[16,16]{1,0:T(8,128)S(1)} %copy-done), custom_call_target="tpu_custom_call" | custom-call | tf_op jit(solution)/shard_map/pallas_call | solution.py:437
  98.8 1.0 copy.8
Async XLA Ops:
  0.7 0.7 copy-start

commit v3 on v2

--- a/solution.py
+++ b/solution.py
@@ -8,7 +8,7 @@
 B = 256
 H = B // 2
 MESH = pl.DeviceIdType.MESH
-N_SEND = 160
+N_SEND = 76
 
 
 def split(values):
@@ -64,9 +64,12 @@
     yes = p >= 0
     sends = []
 
-    def send(cond, src, dst, rsem, dev):
+    slots = {}
+
+    def send(cond, src, dst, rsem, dev, key=None):
+        slot = slots.setdefault(len(sends) if key is None else key, len(slots))
         copy = pltpu.make_async_remote_copy(
-            src_ref=src, dst_ref=dst, send_sem=send_sem.at[len(sends)], recv_sem=rsem,
+            src_ref=src, dst_ref=dst, send_sem=send_sem.at[slot], recv_sem=rsem,
             device_id=dev, device_id_type=MESH,
         )
         sends.append((cond, copy))
@@ -191,8 +194,8 @@
     def red_a(quad, live):
         for half, q in halves:
             src = part.at[quad, pl.ds(half * H, H)]
-            send(live & (q == 0), src, inbox.at[quad, half, 0], red_sem.at[quad, half, 0], toward(1, half))
-            send(live & (q == 3), src, inbox.at[quad, half, 1], red_sem.at[quad, half, 1], toward(2, half))
+            send(live & (q == 0), src, inbox.at[quad, half, 0], red_sem.at[quad, half, 0], toward(1, half), (quad, half))
+            send(live & (q == 3), src, inbox.at[quad, half, 1], red_sem.at[quad, half, 1], toward(2, half), (quad, half))
 
     def red_b(quad, live):
         for half, q in halves:
@@ -204,7 +207,7 @@
                 part[quad, rows] = part[quad, rows] + inbox[quad, half, 1]
 
             src = part.at[quad, rows]
-            send(live & (q == 2), src, inbox.at[quad, half, 1], red_sem.at[quad, half, 1], toward(1, half))
+            send(live & (q == 2), src, inbox.at[quad, half, 1], red_sem.at[quad, half, 1], toward(1, half), (quad, half))
 
     def red_c(quad, live):
         for half, q in halves:
@@ -218,14 +221,14 @@
                 out_ref[orow, ocol] = part[quad, rows] + inbox[quad, half, 0] + inbox[quad, half, 1]
 
             place = out_ref.at[orow, ocol]
-            send(live & (q == 1), place, place, red_sem.at[quad, half, 2], toward(2, half))
-            send(live & (q == 1), place, place, red_sem.at[quad, half, 2], toward(0, half))
+            send(live & (q == 1), place, place, red_sem.at[quad, half, 2], toward(2, half), (quad, half))
+            send(live & (q == 1), place, place, red_sem.at[quad, half, 2], toward(0, half), (quad, half, 2))
 
     def red_d(quad, live):
         for half, q in halves:
             place = out_ref.at[rows_of(quad, half)]
             arrive(live & (q == 2), place, red_sem.at[quad, half, 2])
-            send(live & (q == 2), place, place, red_sem.at[quad, half, 2], toward(3, half))
+            send(live & (q == 2), place, place, red_sem.at[quad, half, 2], toward(3, half), (quad, half, 2))
 
     def red_e(quad, live):
         for half, q in halves:
@@ -418,7 +421,7 @@
     red_e(1, row_live)
     red_e(0, diag_live)
 
-    assert len(sends) <= N_SEND
+    assert len(slots) <= N_SEND
     for cond, copy in sends:
         pl.when(cond)(lambda copy=copy: copy.wait_send())
 

time: 99.9 us -> 99.2 us (level)
  no operation moved by 1% of the time
where the time goes in v3:
time: 99.2 us; the launch traced here: 99 us
  Pallas kernels  96.7 us (97%)
  local copies, waits for them, and re-layouts  1.66 us (2%)
    pallas_call x1, Pallas kernels, local(): pl.pallas_call(kernel, out_shape=jax.ShapeDtypeStruct((2 * B, 2 * B), jnp...  96.7 us

profile of v3, /device:TPU:1, one launch (start us, length us, event | category | flops | bytes accessed | tf_op | source)
XLA Modules:
  0.0 99.0 jit_solution(13939961767089256805)
XLA Ops:
  0.7 0.0 copy-start
  0.7 0.7 copy-done
  1.4 96.7 %shard_map.55 = f32[512,512]{1,0:T(8,128)S(1)} custom-call(f32[1,512,512]{2,1,0:T(8,128)} %low_ref.1, f32[1,512,512]{2,1,0:T(8,128)} %up_ref.1, f32[1,512,512]{2,1,0:T(8,128)} %din_ref.1, f32[1]{0:T(128)S(6)} %copy.7.weight_ref, s32[16,16]{1,0:T(8,128)S(1)} %copy-done), custom_call_target="tpu_custom_call" | custom-call | tf_op jit(solution)/shard_map/pallas_call | solution.py:440
  98.1 1.0 copy.8
Async XLA Ops:
  0.7 0.7 copy-start

commit v4 on v3

--- a/solution.py
+++ b/solution.py
@@ -278,7 +278,6 @@
     arrive(odd_live, row_o.at[jp], ro_sem.at[jp])
     row_send(row_o, ro_sem, needs_o, jp)
     send(row_live, row_u.at[j], row_u.at[j], ru_sem.at[j], partner)
-    row_send(row_u, ru_sem, needs_u, j)
     red_a(3, tt)
 
     la_any = lambda xx: yes
@@ -303,6 +302,7 @@
     for src in (2, 3):
         row_arrive(row_o, ro_sem, needs_o, src)
 
+    row_send(row_u, ru_sem, needs_u, j)
     arrive(row_live, row_u.at[jp], ru_sem.at[jp])
     row_send(row_u, ru_sem, needs_u, jp)
 

time: 99.2 us -> 99.1 us (level)
  no operation moved by 1% of the time
where the time goes in v4:
time: 99.1 us; the launch traced here: 99 us
  Pallas kernels  96.7 us (98%)
  local copies, waits for them, and re-layouts  1.66 us (2%)
    pallas_call x1, Pallas kernels, local(): pl.pallas_call(kernel, out_shape=jax.ShapeDtypeStruct((2 * B, 2 * B), jnp...  96.7 us

profile of v4, /device:TPU:1, one launch (start us, length us, event | category | flops | bytes accessed | tf_op | source)
XLA Modules:
  0.0 99.0 jit_solution(546168744191203416)
XLA Ops:
  0.7 0.0 copy-start
  0.7 0.7 copy-done
  1.4 96.7 %shard_map.55 = f32[512,512]{1,0:T(8,128)S(1)} custom-call(f32[1,512,512]{2,1,0:T(8,128)} %low_ref.1, f32[1,512,512]{2,1,0:T(8,128)} %up_ref.1, f32[1,512,512]{2,1,0:T(8,128)} %din_ref.1, f32[1]{0:T(128)S(6)} %copy.7.weight_ref, s32[16,16]{1,0:T(8,128)S(1)} %copy-done), custom_call_target="tpu_custom_call" | custom-call | tf_op jit(solution)/shard_map/pallas_call | solution.py:440
  98.0 1.0 copy.8
Async XLA Ops:
  0.7 0.7 copy-start
